TPU v7x, 32 devices: a whole 2x2x4 slice. The times are simulated.
32 devices in a mesh: dom: 2 (over y), expert: 8 (over z, x), tensor: 2 (over core).
Axes of the slice: x: 2, y: 2, z: 4, core: 2. Of those that a mesh axis runs over, the one named last changes fastest.
Arguments:
- act: bfloat16 [2048, 2048], P(('dom', 'expert'), 'tensor'), parts along dimension 0, may hold values from -6 to 6
- grad_out: bfloat16 [2048, 2048], P(('dom', 'expert'), 'tensor'), parts along dimension 0, may hold values from -6 to 6
- route_ids: int32 [2048, 2], P(('dom', 'expert')), parts along dimension 0, may hold values from 0 to 15, as said below
- gate_probs: bfloat16 [2048, 2], P(('dom', 'expert')), parts along dimension 0, may hold values from 0.099609375 to 1
- w_gate: bfloat16 [2048, 57344], P(None, ('expert', 'tensor')), may hold values from -0.125 to 0.125
- w_up: bfloat16 [2048, 57344], P(None, ('expert', 'tensor')), may hold values from -0.125 to 0.125
- w_down: bfloat16 [57344, 2048], P(('expert', 'tensor')), may hold values from -0.046875 to 0.046875
Outputs:
- d_act: bfloat16 [2048, 2048], P(('dom', 'expert'), 'tensor'), parts along dimension 0
- d_gate: float32 [2048, 2], P(('dom', 'expert')), parts along dimension 0
- dw_gate: bfloat16 [4096, 57344], P('dom', ('expert', 'tensor')), parts along dimension 0
- dw_up: bfloat16 [4096, 57344], P('dom', ('expert', 'tensor')), parts along dimension 0
- dw_down: bfloat16 [57344, 4096], P(('expert', 'tensor'), 'dom'), parts along dimension 1
There are 2 independent parts, one for each index of `dom`. A program takes and returns all parts, laid end to end along the dimension named above; an argument that names none is the same for every part. Nothing has to cross between parts.
Inputs may be any that keep to these rules, and one draw needn't show every extreme that they name: `route_ids`: the two ids of a token differ. Among the 128 tokens of one index of expert, each id below 4 is named by at most 8 tokens, and one id below 4, the same for all indices, is named by exactly 8 tokens of every index.
All inputs are finite; a program needn't handle non-finite values.
Results may differ from a plain program's by a relative error of at most 0.0051.
Values may be sent and summed in bfloat16 or wider, within the bound.
A program may use at most 192 MiB of HBM per device.

v0:
```python
import jax
import jax.numpy as jnp
from jax import lax
from jax.sharding import PartitionSpec as P

FLIGHT = 4
CAP = 8


def expert_terms(rows_in, grads_in, gate_in, gate_w, up_w, down_w):
    pre_gate = jnp.dot(rows_in, gate_w, preferred_element_type=jnp.float32)
    pre_up = jnp.dot(rows_in, up_w, preferred_element_type=jnp.float32)
    hid_grad = jnp.dot(grads_in, down_w.T, preferred_element_type=jnp.float32)
    squash = jax.nn.sigmoid(pre_gate)
    active = pre_gate * squash
    hidden = active * pre_up
    gate_term = jnp.sum(hidden * hid_grad, axis=1)
    weight = gate_in.astype(jnp.float32)[:, None]
    scaled = weight * hid_grad
    grad_gate = (scaled * pre_up * squash * (1.0 + pre_gate * (1.0 - squash))).astype(jnp.bfloat16)
    grad_up = (scaled * active).astype(jnp.bfloat16)
    hidden_w = (weight * hidden).astype(jnp.bfloat16)
    down_grad = jnp.dot(hidden_w.T, grads_in, preferred_element_type=jnp.float32)
    gate_wgrad = jnp.dot(rows_in.T, grad_gate, preferred_element_type=jnp.float32)
    up_wgrad = jnp.dot(rows_in.T, grad_up, preferred_element_type=jnp.float32)
    input_grad = jnp.dot(grad_gate, gate_w.T, preferred_element_type=jnp.float32) + jnp.dot(
        grad_up, up_w.T, preferred_element_type=jnp.float32
    )
    return (input_grad, gate_term, gate_wgrad, up_wgrad, down_grad)


def local(act, grad_out, route_ids, gate_probs, w_gate, w_up, w_down):
    tok_count = route_ids.shape[0]
    rank_count = lax.axis_size("expert")
    group_size = rank_count // FLIGHT
    window = FLIGHT * CAP
    slot_rows = rank_count * CAP
    paired = route_ids.reshape(-1)
    experts_ids = jnp.arange(FLIGHT, dtype=jnp.int32)
    one_hot = (paired[:, None] == experts_ids[None, :]).astype(jnp.int32)
    before = jnp.cumsum(one_hot, axis=0) - one_hot
    target = paired * CAP + jnp.sum(before * one_hot, axis=1)
    pair_index = jnp.where(paired < FLIGHT, target, window)
    picked = jnp.arange(window, dtype=jnp.int32)[:, None] == target[None, :]
    pick_rows = jnp.sum(picked.reshape(window, tok_count, 2).astype(jnp.bfloat16), axis=2)
    gate_slots = jnp.sum(
        jnp.where(picked, gate_probs.reshape(-1)[None, :].astype(jnp.float32), 0.0), axis=1
    ).astype(jnp.bfloat16)
    gate_send = jnp.broadcast_to(
        gate_slots.reshape(FLIGHT, 1, CAP), (FLIGHT, group_size, CAP)
    ).reshape(rank_count, CAP)

    def spread(source_rows):
        placed = jnp.dot(pick_rows, source_rows, preferred_element_type=jnp.float32).astype(
            jnp.bfloat16
        )
        row_width = source_rows.shape[1]
        return jnp.broadcast_to(
            placed.reshape(FLIGHT, 1, CAP, row_width), (FLIGHT, group_size, CAP, row_width)
        ).reshape(rank_count, CAP, row_width)

    rows_half, grads_half, gate_recv = (
        lax.all_to_all(spread(act), "expert", split_axis=0, concat_axis=0, tiled=True),
        lax.all_to_all(spread(grad_out), "expert", split_axis=0, concat_axis=0, tiled=True),
        lax.all_to_all(gate_send, "expert", split_axis=0, concat_axis=0, tiled=True),
    )
    rows_in, grads_in = (
        lax.all_gather(rows_half.reshape(slot_rows, -1), "tensor", axis=1, tiled=True),
        lax.all_gather(grads_half.reshape(slot_rows, -1), "tensor", axis=1, tiled=True),
    )
    input_grad, gate_term, gate_wgrad, up_wgrad, down_grad = expert_terms(
        rows_in, grads_in, gate_recv.reshape(-1), w_gate, w_up, w_down
    )
    input_half = lax.psum_scatter(input_grad, "tensor", scatter_dimension=1, tiled=True)
    returned, gate_back = (
        lax.all_to_all(
            input_half.reshape(rank_count, CAP, -1),
            "expert",
            split_axis=0,
            concat_axis=0,
            tiled=True,
        ),
        lax.all_to_all(
            gate_term.reshape(rank_count, CAP), "expert", split_axis=0, concat_axis=0, tiled=True
        ),
    )
    merged = jnp.sum(returned.reshape(FLIGHT, group_size, CAP, -1), axis=1).reshape(window, -1)
    padded = jnp.concatenate([merged, jnp.zeros((1, merged.shape[1]), jnp.float32)], axis=0)
    token_grad = jnp.sum(padded[pair_index].reshape(tok_count, 2, -1), axis=1)
    gate_merged = jnp.sum(gate_back.reshape(FLIGHT, group_size, CAP), axis=1).reshape(window)
    gate_padded = jnp.concatenate([gate_merged, jnp.zeros((1,), jnp.float32)], axis=0)
    pair_terms = gate_padded[pair_index]
    d_gate = lax.psum(pair_terms, "tensor").reshape(tok_count, 2)
    return (
        token_grad.astype(jnp.bfloat16),
        d_gate,
        gate_wgrad.astype(jnp.bfloat16),
        up_wgrad.astype(jnp.bfloat16),
        down_grad.astype(jnp.bfloat16),
    )


def solution(mesh):
    return jax.shard_map(
        local,
        mesh=mesh,
        in_specs=(
            P(("dom", "expert"), "tensor"),
            P(("dom", "expert"), "tensor"),
            P(("dom", "expert"), None),
            P(("dom", "expert"), None),
            P(None, ("expert", "tensor")),
            P(None, ("expert", "tensor")),
            P(("expert", "tensor"), None),
        ),
        out_specs=(
            P(("dom", "expert"), "tensor"),
            P(("dom", "expert"), None),
            P("dom", ("expert", "tensor")),
            P("dom", ("expert", "tensor")),
            P(("expert", "tensor"), "dom"),
        ),
        check_vma=False,
    )
```

profile of v0, /device:TPU:0, one launch (start us, length us, event | category | flops | bytes accessed | tf_op | source)
XLA Modules:
  0.0 161.1 jit_solution(9027997850094496124)
XLA Ops:
  7.2 0.0 copy-start
  7.2 0.8 copy.33
  8.0 0.1 reshape.161
  8.2 0.1 eq.47
  8.3 1.2 reduce-window.6
  9.5 0.1 slice.77
  9.6 0.1 copy.35
  9.8 0.1 copy.36
  9.8 0.1 add_bitcast_fusion
  10.0 0.8 copy.37
  10.7 0.1 reshape.174
  10.9 0.1 select_reduce_fusion
  11.0 0.1 convert_element_type.75
  11.1 0.6 copy.38
  11.7 7.3 %all-to-all-start = ((bf16[8,1,8]{2,1,0:T(2,128)(2,1)}), bf16[8,1,8]{2,1,0:T(2,128)(2,1)S(1)}, u32[]{:S(2)}, u32[]{:S(2)}) async-start(bf16[8,1,8]{2,1,0:T(2,128)(2,1)} %copy.38), calls=%async_computation | async-start | bytes 8192 | tf_op jit(solution)/shard_map/all_to_all | solution.py:65
  18.9 0.7 broadcast_compare_fusion
  19.6 0.1 reduce_sum.72
  19.8 0.1 copy.40
  19.9 0.0 copy-done
  19.9 0.2 fusion.1
  20.0 5.3 %all-to-all-done = bf16[8,1,8]{2,1,0:T(2,128)(2,1)S(1)} async-done(((bf16[8,1,8]{2,1,0:T(2,128)(2,1)}), bf16[8,1,8]{2,1,0:T(2,128)(2,1)S(1)}, u32[]{:S(2)}, u32[]{:S(2)}) %all-to-all-start) | async-done | bytes 160 | tf_op jit(solution)/shard_map/all_to_all | solution.py:65
  25.3 0.7 broadcast_in_dim.48
  26.0 3.4 %all-to-all-start.2 = ((bf16[8,8,1024]{2,1,0:T(8,128)(2,1)}), bf16[8,8,1024]{2,1,0:T(8,128)(2,1)S(1)}, u32[]{:S(2)}, u32[]{:S(2)}) async-start(bf16[8,8,1024]{2,1,0:T(8,128)(2,1)} %bitcast.7), calls=%async_computation.2 | async-start | bytes 262144 | tf_op jit(solution)/shard_map/all_to_all | solution.py:63
  29.4 1.1 fusion
  30.5 0.1 copy.41
  30.6 0.2 lt.29
  30.8 0.1 mul.79
  30.9 5.7 %all-to-all-done.2 = bf16[8,8,1024]{2,1,0:T(8,128)(2,1)S(1)} async-done(((bf16[8,8,1024]{2,1,0:T(8,128)(2,1)}), bf16[8,8,1024]{2,1,0:T(8,128)(2,1)S(1)}, u32[]{:S(2)}, u32[]{:S(2)}) %all-to-all-start.2) | async-done | bytes 131104 | tf_op jit(solution)/shard_map/all_to_all | solution.py:63
  36.7 0.7 broadcast_in_dim.46
  37.3 3.4 %all-to-all-start.1 = ((bf16[8,8,1024]{2,1,0:T(8,128)(2,1)}), bf16[8,8,1024]{2,1,0:T(8,128)(2,1)S(1)}, u32[]{:S(2)}, u32[]{:S(2)}) async-start(bf16[8,8,1024]{2,1,0:T(8,128)(2,1)} %bitcast.4), calls=%async_computation.1 | async-start | bytes 262144 | tf_op jit(solution)/shard_map/all_to_all | solution.py:64
  40.7 0.0 reduce-scatter.2.cloned.1.call-start
  40.8 0.1 reshape.175
  40.9 2.0 %all_gather.7 = bf16[64,2048]{1,0:T(8,128)(2,1)S(1)} all-gather(bf16[64,1024]{1,0:T(8,128)(2,1)S(1)} %bitcast.87), channel_id=1, replica_groups=mesh['dom'=2,'expert'=8,'tensor'=2] {'tensor'}, dimensions={1}, use_global_device_ids=true | all-gather | bytes 393216 | tf_op jit(solution)/shard_map/all_gather | solution.py:68
  42.9 5.1 %all-to-all-done.1 = bf16[8,8,1024]{2,1,0:T(8,128)(2,1)S(1)} async-done(((bf16[8,8,1024]{2,1,0:T(8,128)(2,1)}), bf16[8,8,1024]{2,1,0:T(8,128)(2,1)S(1)}, u32[]{:S(2)}, u32[]{:S(2)}) %all-to-all-start.1) | async-done | bytes 131104 | tf_op jit(solution)/shard_map/all_to_all | solution.py:64
  48.0 0.0 copy-start.2
  48.0 2.1 %all_gather.6 = bf16[64,2048]{1,0:T(8,128)(2,1)S(1)} all-gather(bf16[64,1024]{1,0:T(8,128)(2,1)S(1)} %bitcast.88), channel_id=1, replica_groups=mesh['dom'=2,'expert'=8,'tensor'=2] {'tensor'}, dimensions={1}, use_global_device_ids=true | all-gather | bytes 393216 | tf_op jit(solution)/shard_map/all_gather | solution.py:69
  50.1 8.5 %fusion.15 = f32[64,3584]{1,0:T(8,128)S(1)} fusion(bf16[64,2048]{1,0:T(8,128)(2,1)S(1)} %all_gather.7, bf16[2048,3584]{1,0:T(8,128)(2,1)} %param.11), kind=kOutput, calls=%fused_computation.72 | convolution fusion | flops 939524096 | bytes 15859712 | tf_op jit(solution)/shard_map/dot_general | solution.py:11
  58.6 0.0 copy-done.2
  58.6 2.6 %fusion.14 = f32[64,3584]{1,0:T(8,128)S(1)} fusion(bf16[64,2048]{1,0:T(8,128)(2,1)S(1)} %all_gather.7, bf16[2048,3584]{1,0:T(8,128)(2,1)S(1)} %copy-done.2), kind=kOutput, calls=%fused_computation.71 | convolution fusion | flops 939524096 | bytes 15859712 | tf_op jit(solution)/shard_map/dot_general | solution.py:12
  61.3 10.0 %multiply_reduce_fusion = (f32[64]{0:T(128)S(1)}, bf16[64,3584]{1,0:T(8,128)(2,1)S(1)}, bf16[64,3584]{1,0:T(8,128)(2,1)S(1)}) fusion(f32[64,3584]{1,0:T(8,128)S(1)} %fusion.14, f32[64,3584]{1,0:T(8,128)S(1)} %fusion.15, f32[64]{0:T(128)S(1)} %reshape.175, bf16[64,2048]{1,0:T(8,128)(2,1)S(1)} %all_gather.6, bf16[3584,2048]{1,0:T(8,128)(2,1)} %param.13), kind=kOutput, calls=%fused_computation.10 | convolution fusion | flops 943423424 | bytes 17695232 | tf_op jit(solution)/shard_map/dot_general | solution.py:13
  71.3 9.7 %fusion.16 = f32[64,2048]{1,0:T(8,128)S(1)} fusion(bf16[64,3584]{1,0:T(8,128)(2,1)S(1)} %get-tuple-element.21, bf16[2048,3584]{1,0:T(8,128)(2,1)} %param.11), kind=kOutput, calls=%fused_computation.73 | convolution fusion | flops 939524096 | bytes 15663104 | tf_op jit(solution)/shard_map/dot_general | solution.py:26
  81.0 10.5 %convolution_add_fusion = f32[64,2048]{1,0:T(8,128)} fusion(f32[64,2048]{1,0:T(8,128)S(1)} %fusion.16, bf16[64,3584]{1,0:T(8,128)(2,1)S(1)} %get-tuple-element.22, bf16[2048,3584]{1,0:T(8,128)(2,1)} %param.12), kind=kOutput, calls=%fused_computation.4 | convolution fusion | flops 939655168 | bytes 16187392 | tf_op jit(solution)/shard_map/dot_general | solution.py:26
  91.5 0.0 reduce-scatter.2.cloned.1.call-update
  91.5 7.8 %convolution_convert_fusion = bf16[3584,2048]{1,0:T(8,128)(2,1)} fusion(bf16[64,2048]{1,0:T(8,128)(2,1)S(1)} %all_gather.6, f32[64]{0:T(128)S(1)} %reshape.175, f32[64,3584]{1,0:T(8,128)S(1)} %fusion.14, f32[64,3584]{1,0:T(8,128)S(1)} %fusion.15), kind=kOutput, calls=%fused_computation.1 | convolution fusion | flops 948469760 | bytes 16777472 | tf_op jit(solution)/shard_map/dot_general | solution.py:23
  99.3 0.7 all_to_all.26
  100.0 3.3 %all-to-all-start.4 = ((f32[8,1,8]{2,1,0:T(1,128)}), f32[8,1,8]{2,1,0:T(1,128)S(1)}, u32[]{:S(2)}, u32[]{:S(2)}) async-start(f32[8,1,8]{2,1,0:T(1,128)} %bitcast.14), calls=%async_computation.5 | async-start | bytes 8192 | tf_op jit(solution)/shard_map/all_to_all | solution.py:83
  103.3 7.6 %convolution_convert_fusion.1 = bf16[2048,3584]{1,0:T(8,128)(2,1)} fusion(bf16[64,2048]{1,0:T(8,128)(2,1)S(1)} %all_gather.7, bf16[64,3584]{1,0:T(8,128)(2,1)S(1)} %get-tuple-element.22), kind=kOutput, calls=%fused_computation.2 | convolution fusion | flops 946864128 | bytes 15400960 | tf_op jit(solution)/shard_map/dot_general | solution.py:25
  110.9 0.0 all-to-all-done.4
  110.9 0.0 reduce-scatter.2.cloned.1.call-done
  110.9 5.9 %all-to-all-start.3 = ((f32[8,8,1024]{2,1,0:T(8,128)}), f32[8,8,1024]{2,1,0:T(8,128)S(1)}, u32[]{:S(2)}, u32[]{:S(2)}) async-start(f32[8,8,1024]{2,1,0:T(8,128)} %bitcast.90), calls=%async_computation.4 | async-start | bytes 524288 | tf_op jit(solution)/shard_map/all_to_all | solution.py:76
  116.8 0.0 copy-start.1
  116.8 7.6 %convolution_convert_fusion.2 = bf16[2048,3584]{1,0:T(8,128)(2,1)} fusion(bf16[64,2048]{1,0:T(8,128)(2,1)S(1)} %all_gather.7, bf16[64,3584]{1,0:T(8,128)(2,1)S(1)} %get-tuple-element.21), kind=kOutput, calls=%fused_computation.3 | convolution fusion | flops 946864128 | bytes 15400960 | tf_op jit(solution)/shard_map/dot_general | solution.py:24
  124.5 0.1 reshape.172
  124.5 0.7 fusion.13
  125.3 0.7 fusion.12
  126.0 20.1 %compare_select_fusion.1 = f32[256]{0:T(256)S(1)} fusion(s32[256]{0:T(256)S(1)} %bitcast.94, f32[]{:T(128)} %bitcast.16, f32[]{:T(128)} %bitcast.17, f32[]{:T(128)} %bitcast.18, f32[]{:T(128)} %bitcast.19, f32[]{:T(128)} %bitcast.20, f32[]{:T(128)} %bitcast.21, f32[]{:T(128)} %bitcast.22, f32[]{:T(128)} %bitcast.23, f32[]{:T(128)} %bitcast.24, f32[]{:T(128)} %bitcast.25, ...), kind=kLoop, calls=%fused_computation.34 | loop fusion | flops 16384 | bytes 2176 | tf_op jit(solution)/shard_map/gather | solution.py:92
  146.0 0.1 reshape.173
  146.2 3.6 %psum.7 = f32[128,2]{1,0:T(8,128)S(1)} all-reduce(f32[128,2]{1,0:T(8,128)S(1)} %reshape.173), channel_id=1, replica_groups=mesh['dom'=2,'expert'=8,'tensor'=2] {'tensor'}, use_global_device_ids=true, to_apply=%region_10.11 | all-reduce | flops 256 | bytes 2048 | tf_op jit(solution)/shard_map/psum | solution.py:93
  149.8 0.6 copy.43
  150.4 0.0 all-to-all-done.3
  150.5 1.1 gather_fusion
  151.5 0.6 reshape.170
  152.2 2.1 %reduce_sum.76 = bf16[128,1024]{1,0:T(8,128)(2,1)} reduce(f32[128,2,1024]{2,1,0:T(2,128)S(1)} %reshape.170, f32[]{:T(128)} %constant.4.clone.1), dimensions={1}, to_apply=%region_7.8 | reduce | flops 131072 | bytes 1310724 | tf_op jit(solution)/shard_map/reduce_sum | solution.py:89
  154.2 0.0 copy-done.1
  (14 shorter events, 0.2 us)
Async XLA Ops:
  7.2 12.7 %copy-start = (bf16[128,1024]{1,0:T(8,128)(2,1)S(1)}, bf16[128,1024]{1,0:T(8,128)(2,1)}, u32[]{:S(2)}) copy-start(bf16[128,1024]{1,0:T(8,128)(2,1)} %param.7) | copy-start | bytes 786436
  11.7 13.6 %all-to-all-start = ((bf16[8,1,8]{2,1,0:T(2,128)(2,1)}), bf16[8,1,8]{2,1,0:T(2,128)(2,1)S(1)}, u32[]{:S(2)}, u32[]{:S(2)}) async-start(bf16[8,1,8]{2,1,0:T(2,128)(2,1)} %copy.38), calls=%async_computation | async-start | bytes 8192 | tf_op jit(solution)/shard_map/all_to_all | solution.py:65
  26.0 10.7 %all-to-all-start.2 = ((bf16[8,8,1024]{2,1,0:T(8,128)(2,1)}), bf16[8,8,1024]{2,1,0:T(8,128)(2,1)S(1)}, u32[]{:S(2)}, u32[]{:S(2)}) async-start(bf16[8,8,1024]{2,1,0:T(8,128)(2,1)} %bitcast.7), calls=%async_computation.2 | async-start | bytes 262144 | tf_op jit(solution)/shard_map/all_to_all | solution.py:63
  37.3 10.7 %all-to-all-start.1 = ((bf16[8,8,1024]{2,1,0:T(8,128)(2,1)}), bf16[8,8,1024]{2,1,0:T(8,128)(2,1)S(1)}, u32[]{:S(2)}, u32[]{:S(2)}) async-start(bf16[8,8,1024]{2,1,0:T(8,128)(2,1)} %bitcast.4), calls=%async_computation.1 | async-start | bytes 262144 | tf_op jit(solution)/shard_map/all_to_all | solution.py:64
  40.7 70.2 %reduce-scatter.2.cloned.1.call-start = ((), (), s32[]{:S(2)}) async-start(), calls=%async_computation.6 | async-start | bytes 786432 | tf_op jit(solution)/shard_map/reduce_scatter | solution.py:74
  48.0 10.7 %copy-start.2 = (bf16[2048,3584]{1,0:T(8,128)(2,1)S(1)}, bf16[2048,3584]{1,0:T(8,128)(2,1)}, u32[]{:S(2)}) copy-start(bf16[2048,3584]{1,0:T(8,128)(2,1)} %param.12) | copy-start | bytes 44040196
  100.0 10.9 %all-to-all-start.4 = ((f32[8,1,8]{2,1,0:T(1,128)}), f32[8,1,8]{2,1,0:T(1,128)S(1)}, u32[]{:S(2)}, u32[]{:S(2)}) async-start(f32[8,1,8]{2,1,0:T(1,128)} %bitcast.14), calls=%async_computation.5 | async-start | bytes 8192 | tf_op jit(solution)/shard_map/all_to_all | solution.py:83
  110.9 39.5 %all-to-all-start.3 = ((f32[8,8,1024]{2,1,0:T(8,128)}), f32[8,8,1024]{2,1,0:T(8,128)S(1)}, u32[]{:S(2)}, u32[]{:S(2)}) async-start(f32[8,8,1024]{2,1,0:T(8,128)} %bitcast.90), calls=%async_computation.4 | async-start | bytes 524288 | tf_op jit(solution)/shard_map/all_to_all | solution.py:76
  116.8 37.4 %copy-start.1 = (bf16[128,1024]{1,0:T(8,128)(2,1)S(1)}, bf16[128,1024]{1,0:T(8,128)(2,1)}, u32[]{:S(2)}) copy-start(bf16[128,1024]{1,0:T(8,128)(2,1)} %param.7) | copy-start | bytes 786436
Sparse Core Ops, SparseCore 0:
  91.6 5.7 reduce-scatter.1
where the time goes:
time: 162 us; the launch traced here: 161 us
  matrix products  65.6 us (40%)
  other arithmetic  24.4 us (15%)
  starting transfers between devices  23.3 us (14%)
  waiting for transfers between devices  16.2 us (10%)
  between operations  14.2 us (9%)
  local copies, waits for them, and re-layouts  9.71 us (6%)
  blocking collectives  7.68 us (5%)
    gather x1, other arithmetic, local(): pair_terms = gate_padded[pair_index]  20.1 us
    dot_general x1, matrix products, expert_terms(): jnp.dot(grad_up, up_w.T, preferred_element_type=jnp.float32)  10.5 us
    dot_general x1, matrix products, expert_terms(): hid_grad = jnp.dot(grads_in, down_w.T, preferred_element_type=jnp.float32)  10 us
    dot_general x1, matrix products, expert_terms(): jnp.dot(grad_gate, gate_w.T, preferred_element_type=jnp.float32)  9.67 us
    dot_general x1, matrix products, expert_terms(): pre_gate = jnp.dot(rows_in, gate_w, preferred_element_type=jnp.float32)  8.54 us
    dot_general x1, matrix products, expert_terms(): jnp.dot(hidden_w.T, grads_in, preferred_element_type=jnp.float32)  7.85 us
    dot_general x1, matrix products, expert_terms(): up_wgrad = jnp.dot(rows_in.T, grad_up, preferred_element_type=jnp.float32)  7.59 us
    dot_general x1, matrix products, expert_terms(): jnp.dot(rows_in.T, grad_gate, preferred_element_type=jnp.float32)  7.59 us
  transfers between devices with their start and end apart: 6, of which 3 were waited for; matrix products, arithmetic and copies ran while one was open for 30% of the time, Pallas kernels for 0%

commit v1 on v0

v1 whole, which is shorter than its diff:
```python
import functools

import jax
import jax.numpy as jnp
from jax import lax
from jax.experimental import pallas as pl
from jax.experimental.pallas import tpu as pltpu
from jax.sharding import PartitionSpec as P

FLIGHT = 4
CAP = 8
LANES = 128
MESH = pl.DeviceIdType.MESH
F32 = jnp.float32
BF16 = jnp.bfloat16


def dot_nt(a, b):
    return lax.dot_general(a, b, (((1,), (1,)), ((), ())), preferred_element_type=F32)


def iota(shape, dim):
    return lax.broadcasted_iota(jnp.int32, shape, dim)


def chosen(ids_ref, expert, slot):
    rows, toks = expert.shape
    id0 = jnp.broadcast_to(ids_ref[0:1, :], (rows, toks))
    id1 = jnp.broadcast_to(ids_ref[1:2, :], (rows, toks))
    first = id0 == expert
    second = id1 == expert
    member = jnp.where(first | second, 1.0, 0.0)
    earlier = jnp.where(iota((toks, toks), 0) < iota((toks, toks), 1), 1.0, 0.0)
    count = jnp.dot(member.astype(BF16), earlier.astype(BF16), preferred_element_type=F32)
    picked = jnp.where(count == slot.astype(F32), member, 0.0)
    return first, second, picked


def inner_kernel(
    ranks, group, tile, act_ref, grad_ref, ids_ref, gate_ref, wg_hbm, wu_hbm, wd_hbm,
    dact_ref, dgate_ref, rows_ref, grads_ref, gg_ref, gu_ref, hw_ref,
    wg, wu, wd, pay, rx, weight, gacc, send_a, own_a, recv_a, recv_b, acc_c, recv_c,
    wsem, s1, s2, s3, rsem, sa, ra, sb, rb, sc, rc,
):
    rank = lax.axis_index("expert")
    half = lax.axis_index("tensor")
    mine = rank // group
    member = lax.rem(rank, group)
    other = 1 - half
    toks, width = act_ref.shape
    full = width + LANES
    slots = ranks
    rows = slots * CAP
    tiles = wg.shape[0]
    dim = wg.shape[1]

    def weight_copies(j):
        col = pl.ds(pl.multiple_of(j * tile, tile), tile)
        return (
            pltpu.make_async_copy(wg_hbm.at[:, col], wg.at[j], wsem.at[0, j]),
            pltpu.make_async_copy(wu_hbm.at[:, col], wu.at[j], wsem.at[1, j]),
            pltpu.make_async_copy(wd_hbm.at[col, :], wd.at[j], wsem.at[2, j]),
        )

    @pl.loop(0, tiles)
    def _(j):
        for c in weight_copies(j):
            c.start()

    def at_plane(e):
        return {"expert": e * group + member, "tensor": half}

    def at_member(i):
        return {"expert": mine * group + i, "tensor": half}

    partner = {"expert": rank, "tensor": other}
    planes = [lax.rem(mine + d, FLIGHT) for d in range(1, FLIGHT)]
    planes_back = [lax.rem(mine + FLIGHT - d, FLIGHT) for d in range(1, FLIGHT)]
    members = [lax.rem(member + d, group) for d in range(1, group)]
    members_back = [lax.rem(member + group - d, group) for d in range(1, group)]

    barrier = pltpu.get_barrier_semaphore()
    for dev in [at_plane(e) for e in planes] + [at_member(i) for i in members] + [partner]:
        pl.semaphore_signal(barrier, inc=1, device_id=dev, device_id_type=MESH)

    r = iota((FLIGHT * 2 * CAP, toks), 0)
    expert_r = r // (2 * CAP)
    first, second, picked = chosen(ids_ref, expert_r, lax.rem(r, CAP))
    is_act = lax.rem(r // CAP, 2) == 0
    pick_a = jnp.where(is_act, picked, 0.0).astype(BF16)
    pick_g = jnp.where(is_act, 0.0, picked).astype(BF16)
    g0 = jnp.broadcast_to(gate_ref[0:1, :], r.shape)
    g1 = jnp.broadcast_to(gate_ref[1:2, :], r.shape)
    gates = jnp.sum(picked * jnp.where(first, g0, g1), axis=1, keepdims=True)
    packed = jnp.dot(pick_a, act_ref[...], preferred_element_type=F32) + jnp.dot(
        pick_g, grad_ref[...], preferred_element_type=F32
    )
    gate_block = jnp.broadcast_to(gates, (FLIGHT * 2 * CAP, LANES))
    for e in range(FLIGHT):
        at = slice(e * 2 * CAP, (e + 1) * 2 * CAP)
        pay[e, :, 0:width] = packed[at].astype(BF16)
        pay[e, :, width:full] = gate_block[at].astype(BF16)

    pl.semaphore_wait(barrier, FLIGHT - 1 + group - 1 + 1)

    here = member * FLIGHT + mine
    sends = []

    def send(src, dst, ssem, dsem, dev):
        c = pltpu.make_async_remote_copy(
            src_ref=src, dst_ref=dst, send_sem=ssem, recv_sem=dsem, device_id=dev, device_id_type=MESH
        )
        c.start()
        sends.append(c)

    def wait_slot(h, slot):
        pltpu.make_async_copy(rx.at[h, slot], rx.at[h, slot], rsem.at[h, slot]).wait()

    for d, e in enumerate(planes):
        send(pay.at[e], rx.at[half, here], s1.at[d], rsem.at[half, here], at_plane(e))
    rx[half, here] = pay[mine]

    def to_partner(slot):
        send(rx.at[half, slot], rx.at[half, slot], s3.at[slot], rsem.at[half, slot], partner)

    for z in [mine] + planes_back:
        slot = member * FLIGHT + z
        if z is not mine:
            wait_slot(half, slot)
        for d, i in enumerate(members):
            send(rx.at[half, slot], rx.at[half, slot], s2.at[d, z], rsem.at[half, slot], at_member(i))
        to_partner(slot)
    for z in [mine] + planes_back:
        for i in members_back:
            slot = i * FLIGHT + z
            wait_slot(half, slot)
            to_partner(slot)
    for slot in range(slots):
        wait_slot(other, slot)

    a = iota((rows, 2 * rows), 0)
    b = iota((rows, 2 * rows), 1)
    want = (a // CAP) * 2 * CAP + lax.rem(a, CAP)
    take_a = jnp.where(b == want, 1.0, 0.0).astype(BF16)
    take_g = jnp.where(b == want + CAP, 1.0, 0.0).astype(BF16)
    for h in range(2):
        got = rx[h].reshape(2 * rows, full)
        cols = slice(h * width, (h + 1) * width)
        rows_ref[:, cols] = jnp.dot(take_a, got[:, 0:width], preferred_element_type=F32).astype(BF16)
        grads_ref[:, cols] = jnp.dot(take_g, got[:, 0:width], preferred_element_type=F32).astype(BF16)
        if h == 0:
            weight[...] = jnp.dot(take_a, got[:, width:full], preferred_element_type=F32)
    gacc[...] = jnp.zeros_like(gacc)

    def hidden_cols(j):
        return pl.ds(pl.multiple_of(j * tile, tile), tile)

    @pl.loop(0, tiles)
    def _(j):
        for c in weight_copies(j):
            c.wait()
        pre_gate = jnp.dot(rows_ref[...], wg[j], preferred_element_type=F32)
        pre_up = jnp.dot(rows_ref[...], wu[j], preferred_element_type=F32)
        hid_grad = dot_nt(grads_ref[...], wd[j])
        sig = jax.nn.sigmoid(pre_gate)
        active = pre_gate * sig
        hidden = active * pre_up
        gacc[...] += jnp.broadcast_to(jnp.sum(hidden * hid_grad, axis=1, keepdims=True), gacc.shape)
        w = weight[:, 0:1]
        scaled = w * hid_grad
        gg_ref[:, hidden_cols(j)] = (scaled * pre_up * sig * (1.0 + pre_gate * (1.0 - sig))).astype(BF16)
        gu_ref[:, hidden_cols(j)] = (scaled * active).astype(BF16)
        hw_ref[hidden_cols(j), :] = jnp.transpose(w * hidden).astype(BF16)

    def input_terms(h, out):
        at = pl.ds(pl.multiple_of(h * width, width), width)
        out[:, width:full] = gacc[...]
        out[:, 0:width] = jnp.zeros((rows, width), F32)

        @pl.loop(0, tiles)
        def _(j):
            out[:, 0:width] += dot_nt(gg_ref[:, hidden_cols(j)], wg[j, at, :]) + dot_nt(
                gu_ref[:, hidden_cols(j)], wu[j, at, :]
            )

    input_terms(other, send_a)
    send(send_a, recv_a, sa, ra, partner)
    input_terms(half, own_a)
    pltpu.make_async_copy(recv_a, recv_a, ra).wait()
    own_a[...] += recv_a[...]

    span = FLIGHT * CAP

    def member_rows(i):
        return pl.ds(pl.multiple_of(i * span, span), span)

    for d, i in enumerate(members):
        send(own_a.at[member_rows(i)], recv_b.at[member], sb.at[d], rb.at[member], at_member(i))
    total = own_a[member_rows(member), :]
    for i in members_back:
        pltpu.make_async_copy(recv_b.at[i], recv_b.at[i], rb.at[i]).wait()
        total = total + recv_b[i]
    acc_c[...] = total

    def plane_rows(e):
        return pl.ds(pl.multiple_of(e * CAP, CAP), CAP)

    for d, e in enumerate(planes):
        send(acc_c.at[plane_rows(e)], recv_c.at[plane_rows(mine)], sc.at[d], rc.at[mine], at_plane(e))
    recv_c[plane_rows(mine), :] = acc_c[plane_rows(mine), :]

    r = iota((span, toks), 0)
    first, second, picked = chosen(ids_ref, r // CAP, lax.rem(r, CAP))
    for e in planes_back:
        part = recv_c.at[plane_rows(e)]
        pltpu.make_async_copy(part, part, rc.at[e]).wait()
    dact_ref[...] = lax.dot_general(
        picked, recv_c[:, 0:width], (((0,), (0,)), ((), ())),
        precision=lax.Precision.HIGHEST, preferred_element_type=F32,
    ).astype(BF16)
    term = picked * recv_c[:, width:width + 1]
    dgate_ref[0:1, :] = jnp.sum(jnp.where(first, term, 0.0), axis=0, keepdims=True)
    dgate_ref[1:2, :] = jnp.sum(jnp.where(second, term, 0.0), axis=0, keepdims=True)

    for c in sends:
        c.wait_send()


def weight_kernel(chunk, rows_ref, hw_ref, gg_ref, gu_ref, grads_ref, dwg_ref, dwu_ref, dwd_ref):
    rows_t = jnp.transpose(rows_ref[...].astype(F32)).astype(BF16)
    hw_t = hw_ref[...]
    for left, right, out in ((rows_t, gg_ref, dwg_ref), (rows_t, gu_ref, dwu_ref), (hw_t, grads_ref, dwd_ref)):
        cols = out.shape[1]
        step = chunk if cols % chunk == 0 else cols
        for c in range(0, cols, step):
            out[:, c:c + step] = jnp.dot(
                left, right[:, c:c + step], preferred_element_type=F32
            ).astype(BF16)


def local(act, grad_out, route_ids, gate_probs, w_gate, w_up, w_down):
    ranks = lax.axis_size("expert")
    group = ranks // FLIGHT
    toks, width = act.shape
    dim, units = w_gate.shape
    tile = 512 if units % 512 == 0 else units
    tiles = units // tile
    rows = ranks * CAP
    full = width + LANES
    span = FLIGHT * CAP
    vmem = pl.BlockSpec(memory_space=pltpu.VMEM)
    hbm = pl.BlockSpec(memory_space=pl.ANY)
    dma = pltpu.SemaphoreType.DMA
    sds = jax.ShapeDtypeStruct
    d_act, d_gate, rows_in, grads_in, grad_gate, grad_up, hidden_t = pl.pallas_call(
        functools.partial(inner_kernel, ranks, group, tile),
        out_shape=(
            sds((toks, width), BF16), sds((2, toks), F32), sds((rows, dim), BF16), sds((rows, dim), BF16),
            sds((rows, units), BF16), sds((rows, units), BF16), sds((units, rows), BF16),
        ),
        in_specs=[vmem] * 4 + [hbm] * 3,
        out_specs=(vmem,) * 7,
        scratch_shapes=[
            pltpu.VMEM((tiles, dim, tile), BF16),
            pltpu.VMEM((tiles, dim, tile), BF16),
            pltpu.VMEM((tiles, tile, dim), BF16),
            pltpu.VMEM((FLIGHT, 2 * CAP, full), BF16),
            pltpu.VMEM((2, ranks, 2 * CAP, full), BF16),
            pltpu.VMEM((rows, LANES), F32),
            pltpu.VMEM((rows, LANES), F32),
            pltpu.VMEM((rows, full), F32),
            pltpu.VMEM((rows, full), F32),
            pltpu.VMEM((rows, full), F32),
            pltpu.VMEM((group, span, full), F32),
            pltpu.VMEM((span, full), F32),
            pltpu.VMEM((span, full), F32),
            dma((3, tiles)),
            dma((FLIGHT,)),
            dma((group, FLIGHT)),
            dma((ranks,)),
            dma((2, ranks)),
            dma(()),
            dma(()),
            dma((group,)),
            dma((group,)),
            dma((FLIGHT,)),
            dma((FLIGHT,)),
        ],
        compiler_params=pltpu.CompilerParams(
            collective_id=0, has_side_effects=True, vmem_limit_bytes=60 * 1024 * 1024
        ),
        cost_estimate=pl.CostEstimate(
            flops=10 * rows * dim * units, bytes_accessed=6 * dim * units, transcendentals=rows * units
        ),
    )(act, grad_out, route_ids.T, gate_probs.astype(F32).T, w_gate, w_up, w_down)
    steps = 16
    while units % (16 * steps) or dim % (LANES * steps):
        steps //= 2
    dw_gate, dw_up, dw_down = pl.pallas_call(
        functools.partial(weight_kernel, 512),
        grid=(steps,),
        out_shape=(sds((dim, units), BF16), sds((dim, units), BF16), sds((units, dim), BF16)),
        in_specs=[
            pl.BlockSpec((rows, dim // steps), lambda g: (0, g)),
            pl.BlockSpec((units // steps, rows), lambda g: (g, 0)),
            vmem, vmem, vmem,
        ],
        out_specs=(
            pl.BlockSpec((dim // steps, units), lambda g: (g, 0)),
            pl.BlockSpec((dim // steps, units), lambda g: (g, 0)),
            pl.BlockSpec((units // steps, dim), lambda g: (g, 0)),
        ),
        compiler_params=pltpu.CompilerParams(vmem_limit_bytes=48 * 1024 * 1024),
        cost_estimate=pl.CostEstimate(
            flops=6 * rows * dim * units, bytes_accessed=6 * dim * units, transcendentals=0
        ),
    )(rows_in, hidden_t, grad_gate, grad_up, grads_in)
    return (d_act, d_gate.T, dw_gate, dw_up, dw_down)


def solution(mesh):
    return jax.shard_map(
        local,
        mesh=mesh,
        in_specs=(
            P(("dom", "expert"), "tensor"),
            P(("dom", "expert"), "tensor"),
            P(("dom", "expert"), None),
            P(("dom", "expert"), None),
            P(None, ("expert", "tensor")),
            P(None, ("expert", "tensor")),
            P(("expert", "tensor"), None),
        ),
        out_specs=(
            P(("dom", "expert"), "tensor"),
            P(("dom", "expert"), None),
            P("dom", ("expert", "tensor")),
            P("dom", ("expert", "tensor")),
            P(("expert", "tensor"), "dom"),
        ),
        check_vma=False,
    )
```

time: 162 us -> 78.1 us (0.48)
  Pallas kernels: 0 us -> 67.9 us
  matrix products: 65.6 us -> 0 us
  starting transfers between devices: 23.3 us -> 0 us
  other arithmetic: 24.4 us -> 1.22 us
  waiting for transfers between devices: 16.2 us -> 0 us
  between operations: 14.2 us -> 0.65 us
  blocking collectives: 7.68 us -> 0 us
  local copies, waits for them, and re-layouts: 9.71 us -> 8.01 us
    pallas_call x0 -> x2, Pallas kernels: none -> 67.9 us  [the longest x1 49.2 us: local(): pl.pallas_call(functools.partial(inner_kernel, ranks, group, tile), out_s...]
    dot_general x10 -> x0, matrix products: 65.6 us -> none  [the longest x1 10.5 us: expert_terms(): jnp.dot(grad_up, up_w.T, preferred_element_type=jnp.float32)]
    all_to_all x5 -> x0, starting transfers between devices: 23.2 us -> none  [the longest x1 7.25 us: local(): lax.all_to_all(gate_send, 'expert', split_axis=0, concat_axis=0, tiled=True)]
    gather x2 -> x0, other arithmetic: 20.1 us -> none  [the longest x1 20.1 us: local(): pair_terms = gate_padded[pair_index]]
    all_to_all x5 -> x0, waiting for transfers between devices: 16.1 us -> none  [the longest x1 5.71 us: local(): lax.all_to_all(spread(act), 'expert', split_axis=0, concat_axis=0, tiled=...]
    unnamed x8 -> x12, local copies, waits for them, and re-layouts: 1.48 us -> 8.01 us
    all_gather x2 -> x0, blocking collectives: 4.1 us -> none  [the longest x1 2.11 us: local(): lax.all_gather(grads_half.reshape(slot_rows, -1), 'tensor', axis=1, tiled...]
    psum x1 -> x0, blocking collectives: 3.59 us -> none  [local(): d_gate = lax.psum(pair_terms, 'tensor').reshape(tok_count, 2)]
  transfers between devices with their start and end apart: 6 -> 0, of which waited for: 3 -> 0; matrix products, arithmetic and copies ran while one was open for 30% -> 0% of each run, Pallas kernels for 0% -> 0%
where the time goes in v1:
time: 78.1 us; the launch traced here: 77.7 us
  Pallas kernels  67.9 us (87%)
  local copies, waits for them, and re-layouts  8.01 us (10%)
  other arithmetic  1.22 us (2%)
    pallas_call x1, Pallas kernels, local(): pl.pallas_call(functools.partial(inner_kernel, ranks, group, tile), out_s...  49.2 us
    pallas_call x1, Pallas kernels, local(): pl.pallas_call(functools.partial(weight_kernel, 512), grid=(steps,), out_...  18.7 us
    unnamed x12, local copies, waits for them, and re-layouts  8.01 us

profile of v1, /device:TPU:0, one launch (start us, length us, event | category | flops | bytes accessed | tf_op | source)
XLA Modules:
  0.0 77.7 jit_solution(11940952528226908662)
XLA Ops:
  0.6 1.2 %convert_bitcast_fusion.gate_ref = f32[2,128]{1,0:T(2,128)} fusion(bf16[128,2]{0,1:T(2,128)(2,1)} %param.10), kind=kLoop, calls=%fused_computation | loop fusion | flops 256 | bytes 1536 | tf_op jit(solution)/shard_map/transpose | solution.py:295
  1.9 49.2 %shard_map.110 = (bf16[128,1024]{1,0:T(8,128)(2,1)}, f32[2,128]{1,0:T(2,128)}, bf16[64,2048]{1,0:T(8,128)(2,1)}, bf16[64,2048]{1,0:T(8,128)(2,1)}, bf16[64,3584]...) custom-call(bf16[128,1024]{1,0:T(8,128)(2,1)} %act_ref.1, bf16[128,1024]{1,0:T(8,128)(2,1)} %grad_ref.1, ...), custom_call_target="tpu_custom_call" | custom-call | flops 4697620480 | bytes 44040192 | tf_op jit(solution)/shard_map/pallas_call | solution.py:255
  51.1 0.0 copy-start
  51.1 1.2 %copy-done = bf16[3584,64]{1,0:T(8,128)(2,1)S(1)} copy-done((bf16[3584,64]{1,0:T(8,128)(2,1)S(1)}, bf16[3584,64]{1,0:T(8,128)(2,1)}, u32[]{:S(2)}) %copy-start) | copy-done | bytes 458776
  52.2 0.0 copy-start.1
  52.2 1.0 %copy-done.1 = bf16[64,3584]{1,0:T(8,128)(2,1)S(1)} copy-done((bf16[64,3584]{1,0:T(8,128)(2,1)S(1)}, bf16[64,3584]{1,0:T(8,128)(2,1)}, u32[]{:S(2)}) %copy-start.1) | copy-done | bytes 458776
  53.3 0.0 copy-start.2
  53.3 1.0 %copy-done.2 = bf16[64,3584]{1,0:T(8,128)(2,1)S(1)} copy-done((bf16[64,3584]{1,0:T(8,128)(2,1)S(1)}, bf16[64,3584]{1,0:T(8,128)(2,1)}, u32[]{:S(2)}) %copy-start.2) | copy-done | bytes 458776
  54.3 0.0 copy-start.3
  54.3 0.9 %copy-done.3 = bf16[64,2048]{1,0:T(8,128)(2,1)S(1)} copy-done((bf16[64,2048]{1,0:T(8,128)(2,1)S(1)}, bf16[64,2048]{1,0:T(8,128)(2,1)}, u32[]{:S(2)}) %copy-start.3) | copy-done | bytes 262168
  55.2 0.0 copy-start.4
  55.2 0.9 %copy-done.4 = bf16[64,2048]{1,0:T(8,128)(2,1)S(1)} copy-done((bf16[64,2048]{1,0:T(8,128)(2,1)S(1)}, bf16[64,2048]{1,0:T(8,128)(2,1)}, u32[]{:S(2)}) %copy-start.4) | copy-done | bytes 262168
  56.2 18.7 %shard_map.111 = (bf16[2048,3584]{1,0:T(8,128)(2,1)}, bf16[2048,3584]{1,0:T(8,128)(2,1)}, bf16[3584,2048]{1,0:T(8,128)(2,1)}) custom-call(bf16[64,2048]{1,0:T(8,128)(2,1)S(1)} %copy-done.3, bf16[3584,64]{1,0:T(8,128)(2,1)S(1)} %copy-done, bf16[64,3584]{1,0:T(8,128)(2,1)S(1)} %copy-done.1, bf16[64,3584]{1,0:T(8,128)(2,1)S(1)} %copy-done.2, ...), custom_call_target="tpu_custom_call" | custom-call | flops 2818572288 | bytes 44040192 | tf_op jit(solution)/shard_map/pallas_call | solution.py:299
  74.8 1.7 %copy.14 = bf16[128,1024]{1,0:T(8,128)(2,1)} copy(bf16[128,1024]{1,0:T(8,128)(2,1)} %get-tuple-element.30) | data formatting | bytes 524288
  76.5 1.2 %copy.15 = f32[128,2]{0,1:T(2,128)} copy(f32[128,2]{0,1:T(2,128)} %bitcast.5) | data formatting | bytes 2048
Async XLA Ops:
  51.1 1.2 %copy-start = (bf16[3584,64]{1,0:T(8,128)(2,1)S(1)}, bf16[3584,64]{1,0:T(8,128)(2,1)}, u32[]{:S(2)}) copy-start(bf16[3584,64]{1,0:T(8,128)(2,1)} %get-tuple-element.18.hw_ref) | copy-start | bytes 1376260
  52.2 1.0 %copy-start.1 = (bf16[64,3584]{1,0:T(8,128)(2,1)S(1)}, bf16[64,3584]{1,0:T(8,128)(2,1)}, u32[]{:S(2)}) copy-start(bf16[64,3584]{1,0:T(8,128)(2,1)} %get-tuple-element.19.gg_ref) | copy-start | bytes 1376260
  53.3 1.0 %copy-start.2 = (bf16[64,3584]{1,0:T(8,128)(2,1)S(1)}, bf16[64,3584]{1,0:T(8,128)(2,1)}, u32[]{:S(2)}) copy-start(bf16[64,3584]{1,0:T(8,128)(2,1)} %get-tuple-element.20.gu_ref) | copy-start | bytes 1376260
  54.3 0.9 %copy-start.3 = (bf16[64,2048]{1,0:T(8,128)(2,1)S(1)}, bf16[64,2048]{1,0:T(8,128)(2,1)}, u32[]{:S(2)}) copy-start(bf16[64,2048]{1,0:T(8,128)(2,1)} %get-tuple-element.17.rows_ref) | copy-start | bytes 786436
  55.2 0.9 %copy-start.4 = (bf16[64,2048]{1,0:T(8,128)(2,1)S(1)}, bf16[64,2048]{1,0:T(8,128)(2,1)}, u32[]{:S(2)}) copy-start(bf16[64,2048]{1,0:T(8,128)(2,1)} %get-tuple-element.21.grads_ref) | copy-start | bytes 786436

commit v2 on v1

--- a/solution.py
+++ b/solution.py
@@ -38,9 +38,9 @@
 
 def inner_kernel(
     ranks, group, tile, act_ref, grad_ref, ids_ref, gate_ref, wg_hbm, wu_hbm, wd_hbm,
-    dact_ref, dgate_ref, rows_ref, grads_ref, gg_ref, gu_ref, hw_ref,
-    wg, wu, wd, pay, rx, weight, gacc, send_a, own_a, recv_a, recv_b, acc_c, recv_c,
-    wsem, s1, s2, s3, rsem, sa, ra, sb, rb, sc, rc,
+    keep_ref, give_ref, rows_ref, grads_ref, gg_ref, gu_ref, hw_ref,
+    wg, wu, wd, pay, rx, weight, gacc, send_a, own_a, recv_a,
+    wsem, s1, s2, s3, rsem, sa, ra,
 ):
     rank = lax.axis_index("expert")
     half = lax.axis_index("tensor")
@@ -89,8 +89,9 @@
     is_act = lax.rem(r // CAP, 2) == 0
     pick_a = jnp.where(is_act, picked, 0.0).astype(BF16)
     pick_g = jnp.where(is_act, 0.0, picked).astype(BF16)
-    g0 = jnp.broadcast_to(gate_ref[0:1, :], r.shape)
-    g1 = jnp.broadcast_to(gate_ref[1:2, :], r.shape)
+    probs = gate_ref[...].astype(F32)
+    g0 = jnp.broadcast_to(probs[0:1, :], r.shape)
+    g1 = jnp.broadcast_to(probs[1:2, :], r.shape)
     gates = jnp.sum(picked * jnp.where(first, g0, g1), axis=1, keepdims=True)
     packed = jnp.dot(pick_a, act_ref[...], preferred_element_type=F32) + jnp.dot(
         pick_g, grad_ref[...], preferred_element_type=F32
@@ -187,55 +188,78 @@
     send(send_a, recv_a, sa, ra, partner)
     input_terms(half, own_a)
     pltpu.make_async_copy(recv_a, recv_a, ra).wait()
-    own_a[...] += recv_a[...]
-
     span = FLIGHT * CAP
 
-    def member_rows(i):
-        return pl.ds(pl.multiple_of(i * span, span), span)
-
+    def both(i):
+        at = pl.ds(pl.multiple_of(i * span, span), span)
+        return own_a[at, :] + recv_a[at, :]
+
+    keep_ref[...] = both(member)
     for d, i in enumerate(members):
-        send(own_a.at[member_rows(i)], recv_b.at[member], sb.at[d], rb.at[member], at_member(i))
-    total = own_a[member_rows(member), :]
-    for i in members_back:
-        pltpu.make_async_copy(recv_b.at[i], recv_b.at[i], rb.at[i]).wait()
-        total = total + recv_b[i]
-    acc_c[...] = total
-
-    def plane_rows(e):
-        return pl.ds(pl.multiple_of(e * CAP, CAP), CAP)
-
-    for d, e in enumerate(planes):
-        send(acc_c.at[plane_rows(e)], recv_c.at[plane_rows(mine)], sc.at[d], rc.at[mine], at_plane(e))
-    recv_c[plane_rows(mine), :] = acc_c[plane_rows(mine), :]
-
-    r = iota((span, toks), 0)
+        give_ref[d] = both(i)
+
+    for c in sends:
+        c.wait_send()
+
+
+def middle_kernel(group, keep_ref, *refs):
+    got, outs = refs[:-FLIGHT], refs[-FLIGHT:]
+    mine = lax.axis_index("expert") // group
+    for d, out in enumerate(outs):
+        at = pl.ds(pl.multiple_of(lax.rem(mine + d, FLIGHT) * CAP, CAP), CAP)
+        total = keep_ref[at, :]
+        for g in got:
+            total = total + g[at, :]
+        out[...] = total
+
+
+def token_kernel(group, ids_ref, *refs):
+    parts, (dact_ref, dgate_ref, back) = refs[:FLIGHT], refs[FLIGHT:]
+    mine = lax.axis_index("expert") // group
+    width = dact_ref.shape[1]
+    for d, part in enumerate(parts):
+        at = pl.ds(pl.multiple_of(lax.rem(mine + FLIGHT - d, FLIGHT) * CAP, CAP), CAP)
+        back[at, :] = part[...]
+    r = iota((FLIGHT * CAP, dact_ref.shape[0]), 0)
     first, second, picked = chosen(ids_ref, r // CAP, lax.rem(r, CAP))
-    for e in planes_back:
-        part = recv_c.at[plane_rows(e)]
-        pltpu.make_async_copy(part, part, rc.at[e]).wait()
     dact_ref[...] = lax.dot_general(
-        picked, recv_c[:, 0:width], (((0,), (0,)), ((), ())),
+        picked, back[:, 0:width], (((0,), (0,)), ((), ())),
         precision=lax.Precision.HIGHEST, preferred_element_type=F32,
     ).astype(BF16)
-    term = picked * recv_c[:, width:width + 1]
+    term = picked * back[:, width:width + 1]
     dgate_ref[0:1, :] = jnp.sum(jnp.where(first, term, 0.0), axis=0, keepdims=True)
     dgate_ref[1:2, :] = jnp.sum(jnp.where(second, term, 0.0), axis=0, keepdims=True)
 
-    for c in sends:
-        c.wait_send()
-
-
-def weight_kernel(chunk, rows_ref, hw_ref, gg_ref, gu_ref, grads_ref, dwg_ref, dwu_ref, dwd_ref):
-    rows_t = jnp.transpose(rows_ref[...].astype(F32)).astype(BF16)
-    hw_t = hw_ref[...]
-    for left, right, out in ((rows_t, gg_ref, dwg_ref), (rows_t, gu_ref, dwu_ref), (hw_t, grads_ref, dwd_ref)):
-        cols = out.shape[1]
-        step = chunk if cols % chunk == 0 else cols
-        for c in range(0, cols, step):
-            out[:, c:c + step] = jnp.dot(
-                left, right[:, c:c + step], preferred_element_type=F32
-            ).astype(BF16)
+
+def weight_kernel(chunk, turn, left_ref, right_ref, out):
+    left = left_ref[...]
+    if turn:
+        left = jnp.transpose(left.astype(F32)).astype(BF16)
+    cols = out.shape[1]
+    step = chunk if cols % chunk == 0 else cols
+    for c in range(0, cols, step):
+        out[:, c:c + step] = jnp.dot(left, right_ref[:, c:c + step], preferred_element_type=F32).astype(BF16)
+
+
+def weight_grad(left, right, turn, steps, vmem_limit):
+    depth, cols = right.shape
+    count = left.shape[1] if turn else left.shape[0]
+    block = count // steps
+    if turn:
+        left_spec = pl.BlockSpec((depth, block), lambda g: (0, g))
+    else:
+        left_spec = pl.BlockSpec((block, depth), lambda g: (g, 0))
+    return pl.pallas_call(
+        functools.partial(weight_kernel, 512, turn),
+        grid=(steps,),
+        out_shape=jax.ShapeDtypeStruct((count, cols), BF16),
+        in_specs=[left_spec, pl.BlockSpec((depth, cols), lambda g: (0, 0))],
+        out_specs=pl.BlockSpec((block, cols), lambda g: (g, 0)),
+        compiler_params=pltpu.CompilerParams(vmem_limit_bytes=vmem_limit),
+        cost_estimate=pl.CostEstimate(
+            flops=8 * depth * count * cols, bytes_accessed=4 * count * cols, transcendentals=0
+        ),
+    )(left, right)
 
 
 def local(act, grad_out, route_ids, gate_probs, w_gate, w_up, w_down):
@@ -252,10 +276,10 @@
     hbm = pl.BlockSpec(memory_space=pl.ANY)
     dma = pltpu.SemaphoreType.DMA
     sds = jax.ShapeDtypeStruct
-    d_act, d_gate, rows_in, grads_in, grad_gate, grad_up, hidden_t = pl.pallas_call(
+    keep, give, rows_in, grads_in, grad_gate, grad_up, hidden_t = pl.pallas_call(
         functools.partial(inner_kernel, ranks, group, tile),
         out_shape=(
-            sds((toks, width), BF16), sds((2, toks), F32), sds((rows, dim), BF16), sds((rows, dim), BF16),
+            sds((span, full), F32), sds((max(group - 1, 1), span, full), F32), sds((rows, dim), BF16), sds((rows, dim), BF16),
             sds((rows, units), BF16), sds((rows, units), BF16), sds((units, rows), BF16),
         ),
         in_specs=[vmem] * 4 + [hbm] * 3,
@@ -271,9 +295,6 @@
             pltpu.VMEM((rows, full), F32),
             pltpu.VMEM((rows, full), F32),
             pltpu.VMEM((rows, full), F32),
-            pltpu.VMEM((group, span, full), F32),
-            pltpu.VMEM((span, full), F32),
-            pltpu.VMEM((span, full), F32),
             dma((3, tiles)),
             dma((FLIGHT,)),
             dma((group, FLIGHT)),
@@ -281,10 +302,6 @@
             dma((2, ranks)),
             dma(()),
             dma(()),
-            dma((group,)),
-            dma((group,)),
-            dma((FLIGHT,)),
-            dma((FLIGHT,)),
         ],
         compiler_params=pltpu.CompilerParams(
             collective_id=0, has_side_effects=True, vmem_limit_bytes=60 * 1024 * 1024
@@ -292,29 +309,36 @@
         cost_estimate=pl.CostEstimate(
             flops=10 * rows * dim * units, bytes_accessed=6 * dim * units, transcendentals=rows * units
         ),
-    )(act, grad_out, route_ids.T, gate_probs.astype(F32).T, w_gate, w_up, w_down)
-    steps = 16
+    )(act, grad_out, route_ids.T, gate_probs.T, w_gate, w_up, w_down)
+    steps = 8
     while units % (16 * steps) or dim % (LANES * steps):
         steps //= 2
-    dw_gate, dw_up, dw_down = pl.pallas_call(
-        functools.partial(weight_kernel, 512),
-        grid=(steps,),
-        out_shape=(sds((dim, units), BF16), sds((dim, units), BF16), sds((units, dim), BF16)),
-        in_specs=[
-            pl.BlockSpec((rows, dim // steps), lambda g: (0, g)),
-            pl.BlockSpec((units // steps, rows), lambda g: (g, 0)),
-            vmem, vmem, vmem,
-        ],
-        out_specs=(
-            pl.BlockSpec((dim // steps, units), lambda g: (g, 0)),
-            pl.BlockSpec((dim // steps, units), lambda g: (g, 0)),
-            pl.BlockSpec((units // steps, dim), lambda g: (g, 0)),
-        ),
-        compiler_params=pltpu.CompilerParams(vmem_limit_bytes=48 * 1024 * 1024),
-        cost_estimate=pl.CostEstimate(
-            flops=6 * rows * dim * units, bytes_accessed=6 * dim * units, transcendentals=0
-        ),
-    )(rows_in, hidden_t, grad_gate, grad_up, grads_in)
+    limit = 60 * 1024 * 1024
+
+    def member_step(d):
+        return [(r, r // group * group + (r % group + d) % group) for r in range(ranks)]
+
+    def plane_step(d):
+        return [(r, ((r // group + d) % FLIGHT) * group + r % group) for r in range(ranks)]
+
+    got = [lax.ppermute(give[d - 1], "expert", member_step(d)) for d in range(1, group)]
+    dw_gate = weight_grad(rows_in, grad_gate, True, steps, limit)
+    parts = pl.pallas_call(
+        functools.partial(middle_kernel, group),
+        out_shape=(sds((CAP, full), F32),) * FLIGHT,
+        in_specs=[vmem] * (1 + len(got)),
+        out_specs=(vmem,) * FLIGHT,
+    )(keep, *got)
+    back = [parts[0]] + [lax.ppermute(parts[d], "expert", plane_step(d)) for d in range(1, FLIGHT)]
+    dw_up = weight_grad(rows_in, grad_up, True, steps, limit)
+    dw_down = weight_grad(hidden_t, grads_in, False, steps, limit)
+    d_act, d_gate = pl.pallas_call(
+        functools.partial(token_kernel, group),
+        out_shape=(sds((toks, width), BF16), sds((2, toks), F32)),
+        in_specs=[vmem] * (1 + FLIGHT),
+        out_specs=(vmem, vmem),
+        scratch_shapes=[pltpu.VMEM((span, full), F32)],
+    )(route_ids.T, *back)
     return (d_act, d_gate.T, dw_gate, dw_up, dw_down)
 
 

time: 78.1 us -> 78.5 us (level)
  local copies, waits for them, and re-layouts: 8.01 us -> 1.27 us
  starting transfers between devices: 0 us -> 5.1 us
  Pallas kernels: 67.9 us -> 70.5 us
  other arithmetic: 1.22 us -> 0 us
    pallas_call x1 -> x5, Pallas kernels: 18.7 us -> 32.3 us  [the longest x3 28.3 us: weight_grad(): pl.pallas_call(functools.partial(weight_kernel, 512, turn), grid=(steps,)...]
    pallas_call x1, Pallas kernels: 49.2 us -> 38.2 us  [local(): pl.pallas_call(functools.partial(inner_kernel, ranks, group, tile), out_s...]
    unnamed x12 -> x8, local copies, waits for them, and re-layouts: 8.01 us -> 1.27 us
    ppermute x0 -> x4, starting transfers between devices: none -> 5.1 us  [the longest x3 4.31 us: local(): lax.ppermute(parts[d], 'expert', plane_step(d))]
    transpose x1 -> x0, other arithmetic: 1.22 us -> none  [local(): gate_probs.astype(F32)]
  transfers between devices with their start and end apart: 0 -> 4, of which waited for: 0 -> 0; matrix products, arithmetic and copies ran while one was open for 0% -> 0% of each run, Pallas kernels for 0% -> 36%
where the time goes in v2:
time: 78.5 us; the launch traced here: 77.6 us
  Pallas kernels  70.5 us (90%)
  starting transfers between devices  5.1 us (6%)
  local copies, waits for them, and re-layouts  1.27 us (2%)
    pallas_call x1, Pallas kernels, local(): pl.pallas_call(functools.partial(inner_kernel, ranks, group, tile), out_s...  38.2 us
    pallas_call x3, Pallas kernels, weight_grad(): pl.pallas_call(functools.partial(weight_kernel, 512, turn), grid=(steps,)...  28.3 us
    ppermute x3, starting transfers between devices, local(): lax.ppermute(parts[d], 'expert', plane_step(d))  4.31 us
    pallas_call x1, Pallas kernels, local(): pl.pallas_call(functools.partial(token_kernel, group), out_shape=(sds((to...  2.3 us
    pallas_call x1, Pallas kernels, local(): pl.pallas_call(functools.partial(middle_kernel, group), out_shape=(sds((C...  1.65 us
  transfers between devices with their start and end apart: 4, of which 0 were waited for; matrix products, arithmetic and copies ran while one was open for 0% of the time, Pallas kernels for 36%

profile of v2, /device:TPU:0, one launch (start us, length us, event | category | flops | bytes accessed | tf_op | source)
XLA Modules:
  0.0 77.6 jit_solution(12383437636157817915)
XLA Ops:
  0.6 38.2 %shard_map.110 = (f32[32,1152]{1,0:T(8,128)}, f32[1,32,1152]{2,1,0:T(8,128)}, bf16[64,2048]{1,0:T(8,128)(2,1)}, bf16[64,2048]{1,0:T(8,128)(2,1)}, bf16[64,3584]{...) custom-call(bf16[128,1024]{1,0:T(8,128)(2,1)} %act_ref.1, bf16[128,1024]{1,0:T(8,128)(2,1)} %grad_ref.1, ...), custom_call_target="tpu_custom_call" | custom-call | flops 4697620480 | bytes 44040192 | tf_op jit(solution)/shard_map/pallas_call | solution.py:279
  38.9 0.8 %collective-permute-start = (f32[32,1152]{1,0:T(8,128)}, f32[32,1152]{1,0:T(8,128)S(1)}, u32[]{:S(2)}, u32[]{:S(2)}) collective-permute-start(f32[32,1152]{1,0:T(8,128)} %bitcast.7), channel_id=1, source_target_pairs={{0,2},{2,0},{4,6},{6,4},{8,10},{10,8},{12,14},{14,12},{1,3},{3,1},... | collective-permute-start | bytes 442376 | tf_op jit(solution)/shard_map/ppermute | solution.py:324
  39.7 9.5 %shard_map.113 = bf16[2048,3584]{1,0:T(8,128)(2,1)} custom-call(bf16[64,2048]{1,0:T(8,128)(2,1)} %get-tuple-element.26.left_ref, bf16[64,3584]{1,0:T(8,128)(2,1)} %get-tuple-element.27.right_ref), custom_call_target="tpu_custom_call" | custom-call | flops 3758096384 | bytes 29360128 | tf_op jit(solution)/shard_map/pallas_call | solution.py:252
  49.1 9.5 %shard_map.114 = bf16[2048,3584]{1,0:T(8,128)(2,1)} custom-call(bf16[64,2048]{1,0:T(8,128)(2,1)} %get-tuple-element.26.left_ref, bf16[64,3584]{1,0:T(8,128)(2,1)} %get-tuple-element.28.right_ref), custom_call_target="tpu_custom_call" | custom-call | flops 3758096384 | bytes 29360128 | tf_op jit(solution)/shard_map/pallas_call | solution.py:252
  58.6 0.0 collective-permute-done.refs_0_
  58.6 0.0 copy-start
  58.6 0.7 copy-done
  59.2 1.7 %shard_map.111 = (f32[8,1152]{1,0:T(8,128)}, f32[8,1152]{1,0:T(8,128)}, f32[8,1152]{1,0:T(8,128)}, f32[8,1152]{1,0:T(8,128)}) custom-call(f32[32,1152]{1,0:T(8,128)} %get-tuple-element.18.keep_ref, f32[32,1152]{1,0:T(8,128)} %copy-done), custom_call_target="tpu_custom_call" | custom-call | tf_op jit(solution)/shard_map/pallas_call | solution.py:326
  60.9 0.6 collective-permute-start.1
  61.5 2.9 %collective-permute-start.2 = (f32[8,1152]{1,0:T(8,128)}, f32[8,1152]{1,0:T(8,128)S(1)}, u32[]{:S(2)}, u32[]{:S(2)}) collective-permute-start(f32[8,1152]{1,0:T(8,128)} %get-tuple-element.22), channel_id=1, source_target_pairs={{0,8},{2,10},{4,12},{6,14},{8,0},{10,2},{12,4},{14,6},{1,9},{3,11}... | collective-permute-start | bytes 110600 | tf_op jit(solution)/shard_map/ppermute | solution.py:332
  64.4 0.8 %collective-permute-start.3 = (f32[8,1152]{1,0:T(8,128)}, f32[8,1152]{1,0:T(8,128)S(1)}, u32[]{:S(2)}, u32[]{:S(2)}) collective-permute-start(f32[8,1152]{1,0:T(8,128)} %get-tuple-element.23), channel_id=1, source_target_pairs={{0,12},{2,14},{4,0},{6,2},{8,4},{10,6},{12,8},{14,10},{1,13},{3,15... | collective-permute-start | bytes 110600 | tf_op jit(solution)/shard_map/ppermute | solution.py:332
  65.2 9.4 %shard_map.115 = bf16[3584,2048]{1,0:T(8,128)(2,1)} custom-call(bf16[3584,64]{1,0:T(8,128)(2,1)} %get-tuple-element.29.left_ref, bf16[64,2048]{1,0:T(8,128)(2,1)} %get-tuple-element.30.right_ref), custom_call_target="tpu_custom_call" | custom-call | flops 3758096384 | bytes 29360128 | tf_op jit(solution)/shard_map/pallas_call | solution.py:252
  74.6 0.0 collective-permute-done.1.refs_1_
  74.6 0.0 copy-start.1
  74.6 0.0 collective-permute-done.2.refs_2_
  74.6 0.0 copy-start.2
  74.6 0.0 collective-permute-done.3.refs_3_
  74.6 0.0 copy-start.3
  74.6 0.6 copy-done.1
  75.2 0.0 copy-done.2
  75.2 0.0 copy-done.3
  75.3 2.3 %shard_map.112 = (bf16[128,1024]{1,0:T(8,128)(2,1)}, f32[2,128]{1,0:T(2,128)}) custom-call(s32[2,128]{1,0:T(2,128)} %bitcast.5, f32[8,1152]{1,0:T(8,128)} %get-tuple-element.20.refs_0_, f32[8,1152]{1,0:T(8,128)} %copy-done.1, f32[8,1152]{1,0:T(8,128)} %copy-done.2, f32[8,1152]{1,0:T(8,128)} %copy-done.3), custom_call_target="tpu_custom_call" | custom-call | tf_op jit(solution)/shard_map/pallas_call | solution.py:335
Async XLA Ops:
  38.9 19.7 %collective-permute-start = (f32[32,1152]{1,0:T(8,128)}, f32[32,1152]{1,0:T(8,128)S(1)}, u32[]{:S(2)}, u32[]{:S(2)}) collective-permute-start(f32[32,1152]{1,0:T(8,128)} %bitcast.7), channel_id=1, source_target_pairs={{0,2},{2,0},{4,6},{6,4},{8,10},{10,8},{12,14},{14,12},{1,3},{3,1},... | collective-permute-start | bytes 442376 | tf_op jit(solution)/shard_map/ppermute | solution.py:324
  58.6 0.7 copy-start
  60.9 13.7 %collective-permute-start.1 = (f32[8,1152]{1,0:T(8,128)}, f32[8,1152]{1,0:T(8,128)S(1)}, u32[]{:S(2)}, u32[]{:S(2)}) collective-permute-start(f32[8,1152]{1,0:T(8,128)} %get-tuple-element.21), channel_id=1, source_target_pairs={{0,4},{2,6},{4,8},{6,10},{8,12},{10,14},{12,0},{14,2},{1,5},{3,7},... | collective-permute-start | bytes 110600 | tf_op jit(solution)/shard_map/ppermute | solution.py:332
  61.5 13.1 %collective-permute-start.2 = (f32[8,1152]{1,0:T(8,128)}, f32[8,1152]{1,0:T(8,128)S(1)}, u32[]{:S(2)}, u32[]{:S(2)}) collective-permute-start(f32[8,1152]{1,0:T(8,128)} %get-tuple-element.22), channel_id=1, source_target_pairs={{0,8},{2,10},{4,12},{6,14},{8,0},{10,2},{12,4},{14,6},{1,9},{3,11}... | collective-permute-start | bytes 110600 | tf_op jit(solution)/shard_map/ppermute | solution.py:332
  64.4 10.3 %collective-permute-start.3 = (f32[8,1152]{1,0:T(8,128)}, f32[8,1152]{1,0:T(8,128)S(1)}, u32[]{:S(2)}, u32[]{:S(2)}) collective-permute-start(f32[8,1152]{1,0:T(8,128)} %get-tuple-element.23), channel_id=1, source_target_pairs={{0,12},{2,14},{4,0},{6,2},{8,4},{10,6},{12,8},{14,10},{1,13},{3,15... | collective-permute-start | bytes 110600 | tf_op jit(solution)/shard_map/ppermute | solution.py:332
  74.6 0.6 copy-start.1
  74.6 0.6 copy-start.2
  74.6 0.6 copy-start.3

commit v3 on v1

--- a/solution.py
+++ b/solution.py
@@ -38,7 +38,7 @@
 
 def inner_kernel(
     ranks, group, tile, act_ref, grad_ref, ids_ref, gate_ref, wg_hbm, wu_hbm, wd_hbm,
-    dact_ref, dgate_ref, rows_ref, grads_ref, gg_ref, gu_ref, hw_ref,
+    back_ref, rows_ref, grads_ref, gg_ref, gu_ref, hw_ref,
     wg, wu, wd, pay, rx, weight, gacc, send_a, own_a, recv_a, recv_b, acc_c, recv_c,
     wsem, s1, s2, s3, rsem, sa, ra, sb, rb, sc, rc,
 ):
@@ -89,8 +89,9 @@
     is_act = lax.rem(r // CAP, 2) == 0
     pick_a = jnp.where(is_act, picked, 0.0).astype(BF16)
     pick_g = jnp.where(is_act, 0.0, picked).astype(BF16)
-    g0 = jnp.broadcast_to(gate_ref[0:1, :], r.shape)
-    g1 = jnp.broadcast_to(gate_ref[1:2, :], r.shape)
+    probs = gate_ref[...].astype(F32)
+    g0 = jnp.broadcast_to(probs[0:1, :], r.shape)
+    g1 = jnp.broadcast_to(probs[1:2, :], r.shape)
     gates = jnp.sum(picked * jnp.where(first, g0, g1), axis=1, keepdims=True)
     packed = jnp.dot(pick_a, act_ref[...], preferred_element_type=F32) + jnp.dot(
         pick_g, grad_ref[...], preferred_element_type=F32
@@ -209,33 +210,62 @@
         send(acc_c.at[plane_rows(e)], recv_c.at[plane_rows(mine)], sc.at[d], rc.at[mine], at_plane(e))
     recv_c[plane_rows(mine), :] = acc_c[plane_rows(mine), :]
 
-    r = iota((span, toks), 0)
-    first, second, picked = chosen(ids_ref, r // CAP, lax.rem(r, CAP))
     for e in planes_back:
         part = recv_c.at[plane_rows(e)]
         pltpu.make_async_copy(part, part, rc.at[e]).wait()
+    back_ref[...] = recv_c[...]
+
+    for c in sends:
+        c.wait_send()
+
+
+def weight_kernel(
+    chunk, rows_ref, hw_ref, gg_ref, gu_ref, grads_ref, back_ref, ids_ref,
+    dwg_hbm, dwu_hbm, dwd_hbm, dact_ref, dgate_ref, bufg, bufu, bufd, sem,
+):
+    steps = bufg.shape[0]
+
+    def product(left, right_ref, buf, b):
+        cols = buf.shape[2]
+        step = chunk if cols % chunk == 0 else cols
+        for c in range(0, cols, step):
+            buf[b, :, c:c + step] = jnp.dot(
+                left, right_ref[:, c:c + step], preferred_element_type=F32
+            ).astype(BF16)
+
+    def copy(buf, out, which, b):
+        size = buf.shape[1]
+        at = pl.ds(pl.multiple_of(b * size, size), size)
+        return pltpu.make_async_copy(buf.at[b], out.at[at, :], sem.at[which, b])
+
+    @pl.loop(0, steps)
+    def _(b):
+        cols, units = bufg.shape[1], bufd.shape[1]
+        left = rows_ref[:, pl.ds(pl.multiple_of(b * cols, cols), cols)]
+        left = jnp.transpose(left.astype(F32)).astype(BF16)
+        product(left, gg_ref, bufg, b)
+        copy(bufg, dwg_hbm, 0, b).start()
+        product(left, gu_ref, bufu, b)
+        copy(bufu, dwu_hbm, 1, b).start()
+        product(hw_ref[pl.ds(pl.multiple_of(b * units, units), units), :], grads_ref, bufd, b)
+        copy(bufd, dwd_hbm, 2, b).start()
+
+    toks, width = dact_ref.shape
+    r = iota((FLIGHT * CAP, toks), 0)
+    first, second, picked = chosen(ids_ref, r // CAP, lax.rem(r, CAP))
     dact_ref[...] = lax.dot_general(
-        picked, recv_c[:, 0:width], (((0,), (0,)), ((), ())),
+        picked, back_ref[:, 0:width], (((0,), (0,)), ((), ())),
         precision=lax.Precision.HIGHEST, preferred_element_type=F32,
     ).astype(BF16)
-    term = picked * recv_c[:, width:width + 1]
+    term = picked * back_ref[:, width:width + 1]
     dgate_ref[0:1, :] = jnp.sum(jnp.where(first, term, 0.0), axis=0, keepdims=True)
     dgate_ref[1:2, :] = jnp.sum(jnp.where(second, term, 0.0), axis=0, keepdims=True)
 
-    for c in sends:
-        c.wait_send()
-
-
-def weight_kernel(chunk, rows_ref, hw_ref, gg_ref, gu_ref, grads_ref, dwg_ref, dwu_ref, dwd_ref):
-    rows_t = jnp.transpose(rows_ref[...].astype(F32)).astype(BF16)
-    hw_t = hw_ref[...]
-    for left, right, out in ((rows_t, gg_ref, dwg_ref), (rows_t, gu_ref, dwu_ref), (hw_t, grads_ref, dwd_ref)):
-        cols = out.shape[1]
-        step = chunk if cols % chunk == 0 else cols
-        for c in range(0, cols, step):
-            out[:, c:c + step] = jnp.dot(
-                left, right[:, c:c + step], preferred_element_type=F32
-            ).astype(BF16)
+    @pl.loop(0, steps)
+    def _(b):
+        copy(bufg, dwg_hbm, 0, b).wait()
+        copy(bufu, dwu_hbm, 1, b).wait()
+        copy(bufd, dwd_hbm, 2, b).wait()
 
 
 def local(act, grad_out, route_ids, gate_probs, w_gate, w_up, w_down):
@@ -252,14 +282,14 @@
     hbm = pl.BlockSpec(memory_space=pl.ANY)
     dma = pltpu.SemaphoreType.DMA
     sds = jax.ShapeDtypeStruct
-    d_act, d_gate, rows_in, grads_in, grad_gate, grad_up, hidden_t = pl.pallas_call(
+    back, rows_in, grads_in, grad_gate, grad_up, hidden_t = pl.pallas_call(
         functools.partial(inner_kernel, ranks, group, tile),
         out_shape=(
-            sds((toks, width), BF16), sds((2, toks), F32), sds((rows, dim), BF16), sds((rows, dim), BF16),
+            sds((span, full), F32), sds((rows, dim), BF16), sds((rows, dim), BF16),
             sds((rows, units), BF16), sds((rows, units), BF16), sds((units, rows), BF16),
         ),
         in_specs=[vmem] * 4 + [hbm] * 3,
-        out_specs=(vmem,) * 7,
+        out_specs=(vmem,) * 6,
         scratch_shapes=[
             pltpu.VMEM((tiles, dim, tile), BF16),
             pltpu.VMEM((tiles, dim, tile), BF16),
@@ -292,29 +322,29 @@
         cost_estimate=pl.CostEstimate(
             flops=10 * rows * dim * units, bytes_accessed=6 * dim * units, transcendentals=rows * units
         ),
-    )(act, grad_out, route_ids.T, gate_probs.astype(F32).T, w_gate, w_up, w_down)
-    steps = 16
+    )(act, grad_out, route_ids.T, gate_probs.T, w_gate, w_up, w_down)
+    steps = 8
     while units % (16 * steps) or dim % (LANES * steps):
         steps //= 2
-    dw_gate, dw_up, dw_down = pl.pallas_call(
+    dw_gate, dw_up, dw_down, d_act, d_gate = pl.pallas_call(
         functools.partial(weight_kernel, 512),
-        grid=(steps,),
-        out_shape=(sds((dim, units), BF16), sds((dim, units), BF16), sds((units, dim), BF16)),
-        in_specs=[
-            pl.BlockSpec((rows, dim // steps), lambda g: (0, g)),
-            pl.BlockSpec((units // steps, rows), lambda g: (g, 0)),
-            vmem, vmem, vmem,
+        out_shape=(
+            sds((dim, units), BF16), sds((dim, units), BF16), sds((units, dim), BF16),
+            sds((toks, width), BF16), sds((2, toks), F32),
+        ),
+        in_specs=[vmem] * 7,
+        out_specs=(hbm, hbm, hbm, vmem, vmem),
+        scratch_shapes=[
+            pltpu.VMEM((steps, dim // steps, units), BF16),
+            pltpu.VMEM((steps, dim // steps, units), BF16),
+            pltpu.VMEM((steps, units // steps, dim), BF16),
+            dma((3, steps)),
         ],
-        out_specs=(
-            pl.BlockSpec((dim // steps, units), lambda g: (g, 0)),
-            pl.BlockSpec((dim // steps, units), lambda g: (g, 0)),
-            pl.BlockSpec((units // steps, dim), lambda g: (g, 0)),
-        ),
-        compiler_params=pltpu.CompilerParams(vmem_limit_bytes=48 * 1024 * 1024),
+        compiler_params=pltpu.CompilerParams(vmem_limit_bytes=60 * 1024 * 1024),
         cost_estimate=pl.CostEstimate(
             flops=6 * rows * dim * units, bytes_accessed=6 * dim * units, transcendentals=0
         ),
-    )(rows_in, hidden_t, grad_gate, grad_up, grads_in)
+    )(rows_in, hidden_t, grad_gate, grad_up, grads_in, back, route_ids.T)
     return (d_act, d_gate.T, dw_gate, dw_up, dw_down)
 
 

time: 78.1 us -> 66.6 us (0.85)
  local copies, waits for them, and re-layouts: 8.01 us -> 0 us
  Pallas kernels: 67.9 us -> 65.8 us
  other arithmetic: 1.22 us -> 0 us
    unnamed x12 -> x0, local copies, waits for them, and re-layouts: 8.01 us -> none
    pallas_call x1, Pallas kernels: 18.7 us -> 17.3 us  [local(): pl.pallas_call(functools.partial(weight_kernel, 512), out_shape=(sds((dim...]
    transpose x1 -> x0, other arithmetic: 1.22 us -> none  [local(): gate_probs.astype(F32)]
where the time goes in v3:
time: 66.6 us; the launch traced here: 66.4 us
  Pallas kernels  65.8 us (99%)
    pallas_call x1, Pallas kernels, local(): pl.pallas_call(functools.partial(inner_kernel, ranks, group, tile), out_s...  48.5 us
    pallas_call x1, Pallas kernels, local(): pl.pallas_call(functools.partial(weight_kernel, 512), out_shape=(sds((dim...  17.3 us

profile of v3, /device:TPU:0, one launch (start us, length us, event | category | flops | bytes accessed | tf_op | source)
XLA Modules:
  0.0 66.4 jit_solution(6006589917969789931)
XLA Ops:
  0.6 48.5 %shard_map.110 = (f32[32,1152]{1,0:T(8,128)}, bf16[64,2048]{1,0:T(8,128)(2,1)}, bf16[64,2048]{1,0:T(8,128)(2,1)}, bf16[64,3584]{1,0:T(8,128)(2,1)}, bf16[64,3584]{1,0:T(8,128)(2,1)}, /*index=5*/bf16[3584,64]{1,0:T(8,128)(2,1)}) custom-call(bf16[128,1024]{1,0:T(8,128)(2,1)} %act_ref.1, bf16[128,1024]{1,0:T(8,128)(2,1)} %grad_ref.1, s32[2,128]{1,0:T(2,128)} %bitcast.3, ...), custom_call_target="tpu_custom_call" | custom-call | flops 4697620480 | bytes 44040192 | tf_op jit(solution)/shard_map/pallas_call | solution.py:285
  49.1 17.3 %shard_map.111 = (bf16[2048,3584]{1,0:T(8,128)(2,1)}, bf16[2048,3584]{1,0:T(8,128)(2,1)}, bf16[3584,2048]{1,0:T(8,128)(2,1)}, bf16[128,1024]{1,0:T(8,128)(2,1)}, f32[2,128]{1,0:T(2,128)}) custom-call(bf16[64,2048]{1,0:T(8,128)(2,1)} %get-tuple-element.16.rows_ref, bf16[3584,64]{1,0:T(8,128)(2,1)} %get-tuple-element.17.hw_ref, ...), custom_call_target="tpu_custom_call" | custom-call | flops 2818572288 | bytes 44040192 | tf_op jit(solution)/shard_map/pallas_call | solution.py:329
